TPU v7x, 32 devices: a whole 2x2x4 slice. The times are simulated.
32 devices in a mesh: groups: 2 (over x), ctx: 16 (over z, y, core).
Axes of the slice: x: 2, y: 2, z: 4, core: 2. Of those that a mesh axis runs over, the one named last changes fastest.
Arguments:
- queries: bfloat16 [4096, 2048], P(('groups', 'ctx')), parts along dimension 0, may hold values from -90 to 90
- keys: bfloat16 [4096, 128], P(('groups', 'ctx')), parts along dimension 0, may hold values from -6 to 6
- values: bfloat16 [4096, 128], P(('groups', 'ctx')), parts along dimension 0, may hold values from -6 to 6
- cache_lengths: int32 [16], P('groups'), parts along dimension 0, may hold values from 1 to 1024, as said below
- query_lengths: int32 [16], P('groups'), parts along dimension 0, may hold values from 1 to 1024, as said below
Outputs:
- attended: bfloat16 [4096, 2048], P(('groups', 'ctx')), parts along dimension 0
- log_total: float32 [4096, 16], P(('groups', 'ctx')), parts along dimension 0
There are 2 independent parts, one for each index of `groups`. A program takes and returns all parts, laid end to end along the dimension named above; each array names one. Nothing has to cross between parts.
Inputs may be any that keep to these rules, and one draw needn't show every extreme that they name: `cache_lengths`: Positive, summing to 2048; the largest is exactly 1024. `query_lengths`: Positive, summing to 2048; the largest is exactly 1024.
All inputs are finite; a program needn't handle non-finite values.
Results may differ from a plain program's by a relative error of at most 0.0045.
Values may be sent and summed in bfloat16 or wider, within the bound.
A program may use at most 64 MiB of HBM per device.

v0:
```python
import math
import jax
import jax.numpy as jnp
from jax import lax
from jax.sharding import PartitionSpec as P

NEG_FILL = -1e30


def request_of(positions, lengths):
    ends = jnp.cumsum(lengths)[:-1]
    return jnp.sum((positions[:, None] >= ends[None, :]).astype(jnp.int32), axis=1)


def shards(queries, keys, values, cache_lengths, query_lengths):
    q_dev = queries.shape[0]
    width = keys.shape[1]
    heads = queries.shape[1] // width
    here = lax.axis_index("ctx")
    rows = queries.reshape(q_dev * heads, width)
    query_req = request_of(here * q_dev + jnp.arange(q_dev, dtype=jnp.int32), query_lengths)
    row_req = jnp.repeat(query_req, heads)
    scale = width ** (-0.5)

    def attend(carry, key_block, value_block, start):
        positions = start + jnp.arange(key_block.shape[0], dtype=jnp.int32)
        cache_req = request_of(positions, cache_lengths)
        top, total, mixed = carry
        score = jnp.dot(rows, key_block.T, preferred_element_type=jnp.float32) * scale
        mask = (row_req[:, None] == cache_req[None, :]) & True
        score = jnp.where(mask, score, NEG_FILL)
        new_top = jnp.maximum(top, jnp.max(score, axis=1))
        factor = jnp.exp(top - new_top)
        weight = jnp.where(mask, jnp.exp(score - new_top[:, None]), 0.0)
        total = total * factor + jnp.sum(weight, axis=1)
        mixed = mixed * factor[:, None] + jnp.dot(
            weight.astype(jnp.bfloat16), value_block, preferred_element_type=jnp.float32
        )
        return (new_top, total, mixed)

    start_state = (
        jnp.full((q_dev * heads,), NEG_FILL, jnp.float32),
        jnp.zeros((q_dev * heads,), jnp.float32),
        jnp.zeros((q_dev * heads, width), jnp.float32),
    )
    key_piece = lax.all_gather(keys, "ctx", axis=0, tiled=True)
    value_piece = lax.all_gather(values, "ctx", axis=0, tiled=True)
    length = key_piece.shape[0]
    block = math.gcd(length, 1024)
    nblocks = length // block

    def one_step(index, state):
        key_block = lax.dynamic_slice_in_dim(key_piece, index * block, block, 0)
        value_block = lax.dynamic_slice_in_dim(value_piece, index * block, block, 0)
        return attend(state, key_block, value_block, index * block)

    top, total, mixed = lax.fori_loop(0, nblocks, one_step, start_state)
    attended = (mixed / total[:, None]).astype(jnp.bfloat16).reshape(q_dev, heads * width)
    log_total = (top + jnp.log(total)).reshape(q_dev, heads)
    return (attended, log_total)


def solution(mesh):
    in_specs = (
        P(("groups", "ctx"), None),
        P(("groups", "ctx"), None),
        P(("groups", "ctx"), None),
        P("groups"),
        P("groups"),
    )
    out_specs = (P(("groups", "ctx"), None), P(("groups", "ctx"), None))
    return jax.shard_map(shards, mesh=mesh, in_specs=in_specs, out_specs=out_specs, check_vma=False)
```

profile of v0, /device:TPU:0, one launch (start us, length us, event | category | flops | bytes accessed | tf_op | source)
XLA Modules:
  0.0 64.0 jit_solution(3821850923970895720)
XLA Ops:
  0.6 0.8 %reduce-window.15 = s32[8,1]{0,1:T(1,128)S(1)} reduce-window(s32[8,1]{0,1:T(1,128)} %bitcast.30, s32[]{:T(128)} %constant.83.clone.1), window={size=8x1 pad=7_0x0_0}, to_apply=%region_2.3 | reduce-window | flops 56 | bytes 68 | tf_op jit(solution)/shard_map/reduce-window.4
  1.5 0.8 %reduce-window.14 = s32[8,1]{0,1:T(1,128)S(1)} reduce-window(s32[8,1]{0,1:T(1,128)} %bitcast.31, s32[]{:T(128)} %constant.83.clone.1), window={size=8x1 pad=7_0x0_0}, to_apply=%region_0.0 | reduce-window | flops 56 | bytes 68 | tf_op jit(solution)/shard_map/reduce-window
  2.3 0.1 convert_reduce_fusion.1
  2.4 1.3 %reshape.46 = bf16[2048,128]{1,0:T(8,128)(2,1)S(1)} reshape(bf16[128,2048]{1,0:T(8,128)(2,1)} %param.7) | data formatting | bytes 1048576 | tf_op jit(solution)/shard_map/reshape | solution.py:20
  3.7 24.8 %all_gather.6 = bf16[2048,128]{1,0:T(8,128)(2,1)S(1)} all-gather(bf16[128,128]{1,0:T(8,128)(2,1)} %param.8), channel_id=1, replica_groups=mesh['groups'=2,'ctx'=16] {'ctx'}, dimensions={0}, use_global_device_ids=true | all-gather | bytes 557056 | tf_op jit(solution)/shard_map/all_gather | solution.py:46
  28.5 19.1 %all_gather.7 = bf16[2048,128]{1,0:T(8,128)(2,1)S(1)} all-gather(bf16[128,128]{1,0:T(8,128)(2,1)} %param.9), channel_id=1, replica_groups=mesh['groups'=2,'ctx'=16] {'ctx'}, dimensions={0}, use_global_device_ids=true | all-gather | bytes 557056 | tf_op jit(solution)/shard_map/all_gather | solution.py:47
  47.6 14.2 %while.20 = (s32[]{:T(128)}, f32[2048]{0:T(1024)S(1)}, f32[2048]{0:T(1024)S(1)}, f32[2048,128]{1,0:T(8,128)S(1)}, s32[8,1]{0,1:T(1,128)S(1)}, /*index=5*/bf16[20...) while((s32[]{:T(128)}, f32[2048]{0:T(1024)S(1)}, ...), condition=%wide.region_7.8_spmd.clone, body=%wide.region_3.7_spmd.clone.sunk | while | flops 1108114432 | bytes 28517148 | solution.py:57
  47.6 0.1 convert_reduce_fusion.3
  47.7 0.1 broadcast_in_dim.81
  47.8 0.1 eq.93
  47.8 1.3 %fusion.30 = (f32[2048]{0:T(1024)S(1)}, f32[1024,2048]{1,0:T(8,128)S(1)}) fusion(s32[2048]{0:T(1024)S(1)} %eq.93, s32[1024]{0:T(1024)S(1)} %convert_reduce_fusion.3, bf16[2048,128]{1,0:T(8,128)(2,1)S(1)} %get-tuple-element.373, bf16[2048,128]{1,0:T(8,128)(2,1)S(1)} %get-tuple-element.372, s32[]{:T(128)S(6)} %select_n.63), kind=kOutput, calls=%fused_computation.3.clone.1 | convolution fusion | flops 545257472 | bytes 9195524 | tf_op jit(solution)/shard_map/while/body/eval_jaxpr/dot_general | solution.py:29
  49.2 2.7 %fusion.31 = f32[2048]{0:T(1024)S(1)} fusion(f32[1024,2048]{1,0:T(8,128)S(1)} %get-tuple-element.338, f32[2048]{0:T(1024)S(1)} %select_maximum_fusion.2, s32[2048]{0:T(1024)S(1)} %eq.93, s32[1024]{0:T(1024)S(1)} %convert_reduce_fusion.3), kind=kLoop, calls=%fused_computation.5.clone.1 | loop fusion | flops 12580864 | bytes 8417280 | tf_op jit(solution)/shard_map/while/body/eval_jaxpr/reduce_sum | solution.py:35
  51.9 2.8 %fusion.33 = f32[2048,128]{1,0:T(8,128)S(1)} fusion(f32[1024,2048]{1,0:T(8,128)S(1)} %get-tuple-element.338, f32[2048]{0:T(1024)S(1)} %select_maximum_fusion.2, s32[2048]{0:T(1024)S(1)} %eq.93, s32[1024]{0:T(1024)S(1)} %convert_reduce_fusion.3, f32[2048,128]{1,0:T(8,128)S(1)} %get-tuple-element.357, f32[2048]{0:T(1024)S(1)} %get-tuple-element.340, ...), kind=kOutput, calls=%fused_computation.7.clone.1 | convolution fusion | flops 550240256 | bytes 10776581 | tf_op jit(solution)/shard_map/while/body/eval_jaxpr/dot_general | solution.py:36
  54.7 0.1 convert_reduce_fusion.3
  54.8 0.1 broadcast_in_dim.81
  54.9 0.1 eq.93
  55.0 1.3 %fusion.30 = (f32[2048]{0:T(1024)S(1)}, f32[1024,2048]{1,0:T(8,128)S(1)}) fusion(s32[2048]{0:T(1024)S(1)} %eq.93, s32[1024]{0:T(1024)S(1)} %convert_reduce_fusion.3, bf16[2048,128]{1,0:T(8,128)(2,1)S(1)} %get-tuple-element.373, bf16[2048,128]{1,0:T(8,128)(2,1)S(1)} %get-tuple-element.372, s32[]{:T(128)S(6)} %select_n.63), kind=kOutput, calls=%fused_computation.3.clone.1 | convolution fusion | flops 545257472 | bytes 9195524 | tf_op jit(solution)/shard_map/while/body/eval_jaxpr/dot_general | solution.py:29
  56.3 2.7 %fusion.31 = f32[2048]{0:T(1024)S(1)} fusion(f32[1024,2048]{1,0:T(8,128)S(1)} %get-tuple-element.338, f32[2048]{0:T(1024)S(1)} %select_maximum_fusion.2, s32[2048]{0:T(1024)S(1)} %eq.93, s32[1024]{0:T(1024)S(1)} %convert_reduce_fusion.3), kind=kLoop, calls=%fused_computation.5.clone.1 | loop fusion | flops 12580864 | bytes 8417280 | tf_op jit(solution)/shard_map/while/body/eval_jaxpr/reduce_sum | solution.py:35
  59.0 2.8 %fusion.33 = f32[2048,128]{1,0:T(8,128)S(1)} fusion(f32[1024,2048]{1,0:T(8,128)S(1)} %get-tuple-element.338, f32[2048]{0:T(1024)S(1)} %select_maximum_fusion.2, s32[2048]{0:T(1024)S(1)} %eq.93, s32[1024]{0:T(1024)S(1)} %convert_reduce_fusion.3, f32[2048,128]{1,0:T(8,128)S(1)} %get-tuple-element.357, f32[2048]{0:T(1024)S(1)} %get-tuple-element.340, ...), kind=kOutput, calls=%fused_computation.7.clone.1 | convolution fusion | flops 550240256 | bytes 10776581 | tf_op jit(solution)/shard_map/while/body/eval_jaxpr/dot_general | solution.py:36
  61.8 0.3 divide_convert_fusion
  62.2 1.0 %reshape.47 = bf16[128,2048]{1,0:T(8,128)(2,1)} reshape(bf16[2048,128]{1,0:T(8,128)(2,1)S(1)} %divide_convert_fusion) | data formatting | bytes 1048576 | tf_op jit(solution)/shard_map/reshape | solution.py:58
  63.2 0.1 reshape.48
  63.3 0.7 %copy.8 = f32[128,16]{0,1:T(8,128)} copy(f32[128,16]{1,0:T(8,128)S(1)} %reshape.48) | data formatting | bytes 16384
  (16 shorter events, 0.1 us)
where the time goes:
time: 64.2 us; the launch traced here: 64 us
  blocking collectives  43.9 us (68%)
  matrix products  8.24 us (13%)
  other arithmetic  7.64 us (12%)
  local copies, waits for them, and re-layouts  3.38 us (5%)
  between operations  0.68 us (1%)
    all_gather x1, blocking collectives, shards(): key_piece = lax.all_gather(keys, 'ctx', axis=0, tiled=True)  24.8 us
    all_gather x1, blocking collectives, shards(): value_piece = lax.all_gather(values, 'ctx', axis=0, tiled=True)  19.1 us
    dot_general x2, matrix products, attend(): jnp.dot(weight.astype(jnp.bfloat16), value_block, preferred_element_type=...  5.61 us
    reduce_sum x2, other arithmetic, attend(): total = total * factor + jnp.sum(weight, axis=1)  5.33 us
    dot_general x2, matrix products, attend(): jnp.dot(rows, key_block.T, preferred_element_type=jnp.float32) * scale  2.62 us
    another operation x2, other arithmetic  1.66 us

commit v1 on v0

--- a/solution.py
+++ b/solution.py
@@ -43,8 +43,11 @@
         jnp.zeros((q_dev * heads,), jnp.float32),
         jnp.zeros((q_dev * heads, width), jnp.float32),
     )
-    key_piece = lax.all_gather(keys, "ctx", axis=0, tiled=True)
-    value_piece = lax.all_gather(values, "ctx", axis=0, tiled=True)
+    key_piece, value_piece = jnp.split(
+        lax.all_gather(jnp.concatenate([keys, values], axis=1), "ctx", axis=0, tiled=True),
+        [keys.shape[1]],
+        axis=1,
+    )
     length = key_piece.shape[0]
     block = math.gcd(length, 1024)
     nblocks = length // block

time: 64.2 us -> 76.2 us (1.19)
  blocking collectives: 43.9 us -> 0 us
  waiting for transfers between devices: 0 us -> 39.7 us
  between operations: 0.68 us -> 14.1 us
  other arithmetic: 7.64 us -> 9.06 us
  local copies, waits for them, and re-layouts: 3.38 us -> 4.65 us
    all_gather x2 -> x0, blocking collectives: 43.9 us -> none  [the longest x1 24.8 us: shards(): key_piece = lax.all_gather(keys, 'ctx', axis=0, tiled=True)]
    all_gather x0 -> x1, waiting for transfers between devices: none -> 39.7 us  [shards(): lax.all_gather(jnp.concatenate([keys, values], axis=1), 'ctx', axis=0, ti...]
    concatenate x0 -> x1, other arithmetic: none -> 1.41 us  [shards(): jnp.concatenate([keys, values], axis=1)]
    split x0 -> x1, local copies, waits for them, and re-layouts: none -> 1.27 us  [shards(): jnp.split(lax.all_gather(jnp.concatenate([keys, values], axis=1), 'ctx',...]
  transfers between devices with their start and end apart: 0 -> 1, of which waited for: 0 -> 1; matrix products, arithmetic and copies ran while one was open for 0% -> 4% of each run, Pallas kernels for 0% -> 0%
where the time goes in v1:
time: 76.2 us; the launch traced here: 75.9 us
  waiting for transfers between devices  39.7 us (52%)
  between operations  14.1 us (19%)
  other arithmetic  9.06 us (12%)
  matrix products  8.23 us (11%)
  local copies, waits for them, and re-layouts  4.65 us (6%)
    all_gather x1, waiting for transfers between devices, shards(): lax.all_gather(jnp.concatenate([keys, values], axis=1), 'ctx', axis=0, ti...  39.7 us
    dot_general x2, matrix products, attend(): jnp.dot(weight.astype(jnp.bfloat16), value_block, preferred_element_type=...  5.61 us
    reduce_sum x2, other arithmetic, attend(): total = total * factor + jnp.sum(weight, axis=1)  5.33 us
    dot_general x2, matrix products, attend(): jnp.dot(rows, key_block.T, preferred_element_type=jnp.float32) * scale  2.61 us
    another operation x2, other arithmetic  1.66 us
  transfers between devices with their start and end apart: 1, of which 1 were waited for; matrix products, arithmetic and copies ran while one was open for 4% of the time, Pallas kernels for 0%

profile of v1, /device:TPU:0, one launch (start us, length us, event | category | flops | bytes accessed | tf_op | source)
XLA Modules:
  0.0 75.9 jit_solution(14819751488951587506)
XLA Ops:
  7.2 0.0 all-gather.2.cloned.1.call-start
  7.2 1.4 %pad_maximum_fusion = bf16[128,256]{1,0:T(8,128)(2,1)} fusion(bf16[128,128]{1,0:T(8,128)(2,1)} %param.9, bf16[128,128]{1,0:T(8,128)(2,1)} %param.8), kind=kLoop, calls=%fused_computation.25 | loop fusion | flops 131072 | bytes 131072 | tf_op jit(solution)/shard_map/concatenate | solution.py:47
  8.6 0.0 all-gather.2.cloned.1.call-update
  8.7 0.8 %reduce-window.15 = s32[8,1]{0,1:T(1,128)S(1)} reduce-window(s32[8,1]{0,1:T(1,128)} %bitcast.30, s32[]{:T(128)} %constant.83.clone.1), window={size=8x1 pad=7_0x0_0}, to_apply=%region_2.3 | reduce-window | flops 56 | bytes 68 | tf_op jit(solution)/shard_map/reduce-window.4
  9.5 0.8 %reduce-window.14 = s32[8,1]{0,1:T(1,128)S(1)} reduce-window(s32[8,1]{0,1:T(1,128)} %bitcast.31, s32[]{:T(128)} %constant.83.clone.1), window={size=8x1 pad=7_0x0_0}, to_apply=%region_0.0 | reduce-window | flops 56 | bytes 68 | tf_op jit(solution)/shard_map/reduce-window
  10.3 1.3 %reshape.46 = bf16[2048,128]{1,0:T(8,128)(2,1)S(1)} reshape(bf16[128,2048]{1,0:T(8,128)(2,1)} %param.7) | data formatting | bytes 1048576 | tf_op jit(solution)/shard_map/reshape | solution.py:20
  11.7 0.1 convert_reduce_fusion.1
  11.7 39.7 %all-gather.2.cloned.1.call-done = bf16[2048,256]{1,0:T(8,128)(2,1)} async-done(((bf16[128,256]{1,0:T(8,128)(2,1)}), bf16[2048,256]{1,0:T(8,128)(2,1)}) %all-gather.2.cloned.1.call-update) | async-done | bytes 1048592 | tf_op jit(solution)/shard_map/all_gather | solution.py:47
  51.4 1.3 %fusion.19 = (bf16[2048,128]{1,0:T(8,128)(2,1)S(1)}, bf16[2048,128]{1,0:T(8,128)(2,1)S(1)}) fusion(bf16[2048,256]{1,0:T(8,128)(2,1)} %all-gather.2.cloned.1.call-done), kind=kLoop, calls=%fused_computation.30 | loop fusion | bytes 2097152 | tf_op jit(solution)/shard_map/split | solution.py:46
  52.7 14.3 %while.20 = (s32[]{:T(128)}, f32[2048]{0:T(1024)S(1)}, f32[2048]{0:T(1024)S(1)}, f32[2048,128]{1,0:T(8,128)S(1)}, s32[8,1]{0,1:T(1,128)S(1)}, /*index=5*/bf16[20...) while((s32[]{:T(128)}, f32[2048]{0:T(1024)S(1)}, ...), condition=%wide.region_7.8_spmd.clone, body=%wide.region_3.7_spmd.clone.sunk | while | flops 1108114432 | bytes 28517148 | solution.py:60
  52.7 0.1 convert_reduce_fusion.3
  52.8 0.1 broadcast_in_dim.81
  52.9 0.1 eq.93
  53.0 1.3 %fusion.31 = (f32[2048]{0:T(1024)S(1)}, f32[1024,2048]{1,0:T(8,128)S(1)}) fusion(s32[2048]{0:T(1024)S(1)} %eq.93, s32[1024]{0:T(1024)S(1)} %convert_reduce_fusion.3, bf16[2048,128]{1,0:T(8,128)(2,1)S(1)} %get-tuple-element.375, bf16[2048,128]{1,0:T(8,128)(2,1)S(1)} %get-tuple-element.374, s32[]{:T(128)S(6)} %select_n.63), kind=kOutput, calls=%fused_computation.3.clone.1 | convolution fusion | flops 545257472 | bytes 9195524 | tf_op jit(solution)/shard_map/while/body/eval_jaxpr/dot_general | solution.py:29
  54.3 2.7 %fusion.32 = f32[2048]{0:T(1024)S(1)} fusion(f32[1024,2048]{1,0:T(8,128)S(1)} %get-tuple-element.340, f32[2048]{0:T(1024)S(1)} %select_maximum_fusion.2, s32[2048]{0:T(1024)S(1)} %eq.93, s32[1024]{0:T(1024)S(1)} %convert_reduce_fusion.3), kind=kLoop, calls=%fused_computation.5.clone.1 | loop fusion | flops 12580864 | bytes 8417280 | tf_op jit(solution)/shard_map/while/body/eval_jaxpr/reduce_sum | solution.py:35
  57.0 2.8 %fusion.34 = f32[2048,128]{1,0:T(8,128)S(1)} fusion(f32[1024,2048]{1,0:T(8,128)S(1)} %get-tuple-element.340, f32[2048]{0:T(1024)S(1)} %select_maximum_fusion.2, s32[2048]{0:T(1024)S(1)} %eq.93, s32[1024]{0:T(1024)S(1)} %convert_reduce_fusion.3, f32[2048,128]{1,0:T(8,128)S(1)} %get-tuple-element.359, f32[2048]{0:T(1024)S(1)} %get-tuple-element.342, ...), kind=kOutput, calls=%fused_computation.7.clone.1 | convolution fusion | flops 550240256 | bytes 10776581 | tf_op jit(solution)/shard_map/while/body/eval_jaxpr/dot_general | solution.py:36
  59.9 0.1 convert_reduce_fusion.3
  59.9 0.1 broadcast_in_dim.81
  60.0 0.1 eq.93
  60.1 1.3 %fusion.31 = (f32[2048]{0:T(1024)S(1)}, f32[1024,2048]{1,0:T(8,128)S(1)}) fusion(s32[2048]{0:T(1024)S(1)} %eq.93, s32[1024]{0:T(1024)S(1)} %convert_reduce_fusion.3, bf16[2048,128]{1,0:T(8,128)(2,1)S(1)} %get-tuple-element.375, bf16[2048,128]{1,0:T(8,128)(2,1)S(1)} %get-tuple-element.374, s32[]{:T(128)S(6)} %select_n.63), kind=kOutput, calls=%fused_computation.3.clone.1 | convolution fusion | flops 545257472 | bytes 9195524 | tf_op jit(solution)/shard_map/while/body/eval_jaxpr/dot_general | solution.py:29
  61.4 2.7 %fusion.32 = f32[2048]{0:T(1024)S(1)} fusion(f32[1024,2048]{1,0:T(8,128)S(1)} %get-tuple-element.340, f32[2048]{0:T(1024)S(1)} %select_maximum_fusion.2, s32[2048]{0:T(1024)S(1)} %eq.93, s32[1024]{0:T(1024)S(1)} %convert_reduce_fusion.3), kind=kLoop, calls=%fused_computation.5.clone.1 | loop fusion | flops 12580864 | bytes 8417280 | tf_op jit(solution)/shard_map/while/body/eval_jaxpr/reduce_sum | solution.py:35
  64.1 2.8 %fusion.34 = f32[2048,128]{1,0:T(8,128)S(1)} fusion(f32[1024,2048]{1,0:T(8,128)S(1)} %get-tuple-element.340, f32[2048]{0:T(1024)S(1)} %select_maximum_fusion.2, s32[2048]{0:T(1024)S(1)} %eq.93, s32[1024]{0:T(1024)S(1)} %convert_reduce_fusion.3, f32[2048,128]{1,0:T(8,128)S(1)} %get-tuple-element.359, f32[2048]{0:T(1024)S(1)} %get-tuple-element.342, ...), kind=kOutput, calls=%fused_computation.7.clone.1 | convolution fusion | flops 550240256 | bytes 10776581 | tf_op jit(solution)/shard_map/while/body/eval_jaxpr/dot_general | solution.py:36
  67.0 0.3 divide_convert_fusion
  67.3 1.0 %reshape.47 = bf16[128,2048]{1,0:T(8,128)(2,1)} reshape(bf16[2048,128]{1,0:T(8,128)(2,1)S(1)} %divide_convert_fusion) | data formatting | bytes 1048576 | tf_op jit(solution)/shard_map/reshape | solution.py:61
  68.3 0.1 reshape.48
  68.4 0.7 copy.8
  (16 shorter events, 0.1 us)
Async XLA Ops:
  7.2 44.2 %all-gather.2.cloned.1.call-start = ((), (), s32[]{:S(2)}) async-start(), calls=%async_computation | async-start | bytes 1114112 | tf_op jit(solution)/shard_map/all_gather | solution.py:47
Sparse Core Ops, SparseCore 0:
  10.7 40.6 all-gather.1
